TPU v7x, 512 devices: a whole 4x8x8 slice. The times are simulated.
512 devices in a mesh: grp: 16 (over z_lo, x), dev: 32 (over y, z_hi, core).
Axes of the slice: x: 4, y: 8, z: 8 (z_hi: 2, z_lo: 4; z = z_hi * 4 + z_lo), core: 2. Of those that a mesh axis runs over, the one named last changes fastest.
Arguments:
- coeffs: bfloat16 [32768, 1024], P(('grp', 'dev')), may hold values from -6 to 6
- self_blocks: bfloat16 [4, 32768, 1024], P(None, 'grp'), may hold values from -0.75 to 0.75
- cross_blocks: bfloat16 [4, 32768, 1024], P(None, 'grp'), may hold values from -0.75 to 0.75
- pattern: int32 [4, 512, 64], P(None, 'grp'), may hold values from 0 to 63, each once within a row
Outputs:
- result: bfloat16 [32768, 1024], P(('grp', 'dev'))
Inputs may be any that keep to these rules, and one draw needn't show every extreme that they name: Each row pattern[l, p, :] is a permutation of the local box indices.
All inputs are finite; a program needn't handle non-finite values.
Results may differ from a plain program's by a relative error of at most 0.0064.
Values may be sent and summed in bfloat16 or wider, within the bound.
A program may use at most 128 MiB of HBM per device.

v0:
```python
import jax
import jax.numpy as jnp
from jax import lax
from jax.sharding import PartitionSpec as P

R = 32


def from_partner(value, axis, bit):
    mask = 2**bit
    pairs = [(source, source ^ mask) for source in range(lax.axis_size(axis))]
    return lax.ppermute(value, axis, pairs)


def combine(state, self_w, cross_w, picked):
    boxes = state.shape[0]
    own_x = state.reshape(boxes, -1, R)
    other_x = picked.reshape(boxes, -1, R)
    self_m = self_w.reshape(boxes, R, R)
    cross_m = cross_w.reshape(boxes, R, R)
    total = jnp.einsum("bkr,bsr->bks", own_x, self_m, preferred_element_type=jnp.float32)
    total = total + jnp.einsum("bkr,bsr->bks", other_x, cross_m, preferred_element_type=jnp.float32)
    return total.reshape(boxes, -1).astype(jnp.bfloat16)


def device_rows(blocks, level, device, boxes):
    return lax.dynamic_slice_in_dim(blocks[level], device * boxes, boxes, 0)


def device_order(pattern, level, device):
    return lax.dynamic_slice_in_dim(pattern[level], device, 1, 0)[0]


def swap_step(values, outer, bit):
    if outer:
        return from_partner(values, "grp", bit)
    return from_partner(values, "dev", bit)


def level_pair(state, self_blocks, cross_blocks, pattern, first, outer, high_bit):
    boxes = state.shape[0]
    local = lax.axis_index("dev")
    self_one = device_rows(self_blocks, first, local, boxes)
    cross_one = device_rows(cross_blocks, first, local, boxes)
    self_two = device_rows(self_blocks, first + 1, local, boxes)
    cross_two = device_rows(cross_blocks, first + 1, local, boxes)
    order_one = device_order(pattern, first, local)
    order_two = device_order(pattern, first + 1, local)
    near = swap_step(state, outer, high_bit)
    here = combine(state, self_one, cross_one, jnp.take(near, order_one, axis=0))
    there = swap_step(here, outer, 0)
    return combine(here, self_two, cross_two, jnp.take(there, order_two, axis=0))


def shards(coeffs, self_blocks, cross_blocks, pattern):
    inner_high = lax.axis_size("dev").bit_length() - 2
    outer_high = lax.axis_size("grp").bit_length() - 2
    state = level_pair(coeffs, self_blocks, cross_blocks, pattern, 0, False, inner_high)
    state = level_pair(state, self_blocks, cross_blocks, pattern, 2, True, outer_high)
    return state


def solution(mesh):
    return jax.shard_map(
        shards,
        mesh=mesh,
        in_specs=(
            P(("grp", "dev"), None),
            P(None, "grp", None),
            P(None, "grp", None),
            P(None, "grp", None),
        ),
        out_specs=P(("grp", "dev"), None),
        check_vma=False,
    )
```

profile of v0, /device:TPU:1, one launch (start us, length us, event | category | flops | bytes accessed | tf_op | source)
XLA Modules:
  0.0 92.8 jit_solution(17599818642720151592)
XLA Ops:
  0.0 8.3 %collective-permute-start = (bf16[64,1024]{1,0:T(8,128)(2,1)}, bf16[64,1024]{1,0:T(8,128)(2,1)S(1)}, u32[]{:S(2)}, u32[]{:S(2)}) collective-permute-start(bf16[64,1024]{1,0:T(8,128)(2,1)} %param.6), channel_id=1, source_target_pairs={{0,16},{1,17},{2,18},{3,19},{4,20},{5,21},{6,22},{7,23},{8,24},{9,... | collective-permute-start | bytes 393224 | tf_op jit(solution)/shard_map/ppermute | solution.py:12
  8.3 1.1 %copy.44 = bf16[64,1024]{0,1:T(8,128)(2,1)S(1)} copy(bf16[64,1024]{1,0:T(8,128)(2,1)} %param.6) | data formatting | bytes 262144 | tf_op args[0]
  12.1 12.2 %fusion.9 = (bf16[1,2048,1024]{2,1,0:T(8,128)(2,1)}, bf16[1,2048,1024]{2,1,0:T(8,128)(2,1)}, bf16[1,2048,1024]{2,1,0:T(8,128)(2,1)}, bf16[1,2048,1024]{2,1,0:T(8,128)(2,1)}) fusion(bf16[4,2048,1024]{2,1,0:T(8,128)(2,1)} %param.7), kind=kLoop, calls=%fused_computation.45 | loop fusion | bytes 33554432 | tf_op jit(solution)/shard_map/slice | solution.py:27
  24.3 1.0 %constant_dynamic-slice_fusion.8 = (bf16[1,64,1024]{2,1,0:T(8,128)(2,1)S(1)}, bf16[1,64,1024]{2,1,0:T(8,128)(2,1)S(1)}) fusion(bf16[1,2048,1024]{2,1,0:T(8,128)(2,1)} %get-tuple-element.20, s32[]{:T(128)S(6)} %select_n.11, bf16[1,2048,1024]{2,1,0:T(8,128)(2,1)} %get-tuple-element.21), kind=kLoop, calls=%fused_computation.28 | loop fusion | bytes 524292 | tf_op jit(solution)/shard_map/dynamic_slice | solution.py:27
  26.2 8.9 %fusion.8 = (bf16[1,2048,1024]{2,1,0:T(8,128)(2,1)S(1)}, bf16[1,2048,1024]{2,1,0:T(8,128)(2,1)}, bf16[1,2048,1024]{2,1,0:T(8,128)(2,1)S(1)}, bf16[1,2048,1024]{2,1,0:T(8,128)(2,1)S(1)}) fusion(bf16[4,2048,1024]{2,1,0:T(8,128)(2,1)} %param.8), kind=kLoop, calls=%fused_computation.44 | loop fusion | bytes 33554432 | tf_op jit(solution)/shard_map/slice | solution.py:27
  38.2 1.5 %copy.70 = bf16[64,32,32]{2,1,0:T(8,128)(2,1)} copy(bf16[64,32,32]{0,2,1:T(8,128)(2,1)S(1)} %bitcast.61) | data formatting | bytes 262144 | tf_op jit(solution)/shard_map/reshape | solution.py:19
  39.9 1.5 %copy.62 = bf16[64,32,32]{2,1,0:T(8,128)(2,1)} copy(bf16[64,32,32]{0,2,1:T(8,128)(2,1)S(1)} %bitcast.62) | data formatting | bytes 262144 | tf_op jit(solution)/shard_map/reshape | solution.py:19
  41.6 1.5 %copy.55 = bf16[64,32,32]{2,1,0:T(8,128)(2,1)} copy(bf16[64,32,32]{0,2,1:T(8,128)(2,1)S(1)} %bitcast.63) | data formatting | bytes 262144 | tf_op jit(solution)/shard_map/reshape | solution.py:19
  47.0 1.5 %copy.51 = bf16[64,32,32]{2,1,0:T(8,128)(2,1)} copy(bf16[64,32,32]{0,2,1:T(8,128)(2,1)S(1)} %bitcast.66) | data formatting | bytes 262144 | tf_op jit(solution)/shard_map/reshape | solution.py:20
  50.8 1.5 %copy.50 = bf16[64,32,32]{2,1,0:T(8,128)(2,1)} copy(bf16[64,32,32]{0,2,1:T(8,128)(2,1)S(1)} %bitcast.67) | data formatting | bytes 262144 | tf_op jit(solution)/shard_map/reshape | solution.py:18
  52.3 1.6 %fusion.12 = f32[64,32,32]{2,1,0:T(8,128)S(1)} fusion(bf16[64,32,32]{2,1,0:T(8,128)(2,1)} %copy.50, bf16[64,32,32]{2,1,0:T(8,128)(2,1)} %copy.51), kind=kOutput, calls=%fused_computation.48 | convolution fusion | flops 4194304 | bytes 524288 | tf_op jit(solution)/shard_map/bkr,bsr->bks/dot_general | solution.py:22
  53.9 1.4 %copy.52 = f32[64,32,32]{0,2,1:T(8,128)} copy(f32[64,32,32]{2,1,0:T(8,128)S(1)} %fusion.12) | data formatting | bytes 524288 | tf_op jit(solution)/shard_map/bkr,bsr->bks/dot_general | solution.py:22
  55.4 1.1 %fusion.3 = bf16[64,32,32]{0,2,1:T(8,128)(2,1)S(1)} fusion(f32[64,32,32]{0,2,1:T(8,128)} %copy.52, f32[64,32,32]{0,1,2:T(8,128)S(1)} %copy.47), kind=kLoop, calls=%fused_computation.11 | loop fusion | flops 131072 | bytes 655360 | tf_op jit(solution)/shard_map/convert_element_type | solution.py:23
  56.5 1.5 %copy.54 = bf16[64,32,32]{2,1,0:T(8,128)(2,1)} copy(bf16[64,32,32]{0,2,1:T(8,128)(2,1)S(1)} %fusion.3) | data formatting | bytes 262144 | tf_op jit(solution)/shard_map/convert_element_type | solution.py:23
  58.2 3.0 %collective-permute-start.1 = (bf16[64,1024]{1,0:T(8,128)(2,1)S(1)}, bf16[64,1024]{1,0:T(8,128)(2,1)S(1)}, u32[]{:S(2)}, u32[]{:S(2)}) collective-permute-start(bf16[64,1024]{1,0:T(8,128)(2,1)S(1)} %copy.56), channel_id=1, source_target_pairs={{0,1},{1,0},{2,3},{3,2},{4,5},{5,4},{6,7},{7,6},{8,9},{9,8},{10,11... | collective-permute-start | bytes 393224 | tf_op jit(solution)/shard_map/ppermute | solution.py:12
  61.2 1.6 %fusion.13 = f32[64,32,32]{2,1,0:T(8,128)S(1)} fusion(bf16[64,32,32]{2,1,0:T(8,128)(2,1)} %copy.54, bf16[64,32,32]{2,1,0:T(8,128)(2,1)} %copy.55), kind=kOutput, calls=%fused_computation.49 | convolution fusion | flops 4194304 | bytes 524288 | tf_op jit(solution)/shard_map/bkr,bsr->bks/dot_general | solution.py:21
  63.8 1.5 %copy.59 = bf16[64,32,32]{2,1,0:T(8,128)(2,1)} copy(bf16[64,32,32]{0,2,1:T(8,128)(2,1)S(1)} %bitcast.68) | data formatting | bytes 262144 | tf_op jit(solution)/shard_map/reshape | solution.py:18
  65.4 1.4 %fusion = bf16[64,32,32]{2,1,0:T(8,128)(2,1)S(1)} fusion(f32[64,32,32]{2,1,0:T(8,128)S(1)} %fusion.13, bf16[64,32,32]{2,1,0:T(8,128)(2,1)} %copy.59, bf16[64,32,32]{2,1,0:T(8,128)(2,1)S(1)} %copy.60), kind=kOutput, calls=%fused_computation.7 | convolution fusion | flops 4325376 | bytes 655360 | tf_op jit(solution)/shard_map/bkr,bsr->bks/dot_general | solution.py:22
  67.5 5.8 %collective-permute-start.2 = (bf16[64,1024]{1,0:T(8,128)(2,1)S(1)}, bf16[64,1024]{1,0:T(8,128)(2,1)S(1)}, u32[]{:S(2)}, u32[]{:S(2)}) collective-permute-start(bf16[64,1024]{1,0:T(8,128)(2,1)S(1)} %copy.64), channel_id=1, source_target_pairs={{0,256},{32,288},{64,320},{96,352},{128,384},{160,416},{192,448},{... | collective-permute-start | bytes 393224 | tf_op jit(solution)/shard_map/ppermute | solution.py:12
  73.3 1.4 %fusion.14 = f32[64,32,32]{2,1,0:T(8,128)S(1)} fusion(bf16[64,32,32]{2,1,0:T(8,128)(2,1)S(1)} %fusion, bf16[64,32,32]{2,1,0:T(8,128)(2,1)} %copy.62), kind=kOutput, calls=%fused_computation.50 | convolution fusion | flops 4194304 | bytes 524288 | tf_op jit(solution)/shard_map/bkr,bsr->bks/dot_general | solution.py:21
  74.8 5.2 %collective-permute-done.2 = bf16[64,1024]{1,0:T(8,128)(2,1)S(1)} collective-permute-done((bf16[64,1024]{1,0:T(8,128)(2,1)S(1)}, bf16[64,1024]{1,0:T(8,128)(2,1)S(1)}, u32[]{:S(2)}, u32[]{:S(2)}) %collective-permute-start.2) | collective-permute-done | bytes 131104 | tf_op jit(solution)/shard_map/ppermute | solution.py:12
  82.9 3.1 %collective-permute-start.3 = (bf16[64,1024]{1,0:T(8,128)(2,1)S(1)}, bf16[64,1024]{1,0:T(8,128)(2,1)S(1)}, u32[]{:S(2)}, u32[]{:S(2)}) collective-permute-start(bf16[64,1024]{1,0:T(8,128)(2,1)S(1)} %copy.72), channel_id=1, source_target_pairs={{0,32},{32,0},{64,96},{96,64},{128,160},{160,128},{192,224},{224,1... | collective-permute-start | bytes 393224 | tf_op jit(solution)/shard_map/ppermute | solution.py:12
  86.0 1.4 %fusion.15 = f32[64,32,32]{2,1,0:T(8,128)S(1)} fusion(bf16[64,32,32]{2,1,0:T(8,128)(2,1)S(1)} %fusion.1, bf16[64,32,32]{2,1,0:T(8,128)(2,1)} %copy.70), kind=kOutput, calls=%fused_computation.51 | convolution fusion | flops 4194304 | bytes 524288 | tf_op jit(solution)/shard_map/bkr,bsr->bks/dot_general | solution.py:21
  87.4 1.8 %collective-permute-done.3 = bf16[64,1024]{1,0:T(8,128)(2,1)S(1)} collective-permute-done((bf16[64,1024]{1,0:T(8,128)(2,1)S(1)}, bf16[64,1024]{1,0:T(8,128)(2,1)S(1)}, u32[]{:S(2)}, u32[]{:S(2)}) %collective-permute-start.3) | collective-permute-done | bytes 131104 | tf_op jit(solution)/shard_map/ppermute | solution.py:12
  (56 shorter events, 21.2 us)
Async XLA Ops:
  0.0 49.2 %collective-permute-start = (bf16[64,1024]{1,0:T(8,128)(2,1)}, bf16[64,1024]{1,0:T(8,128)(2,1)S(1)}, u32[]{:S(2)}, u32[]{:S(2)}) collective-permute-start(bf16[64,1024]{1,0:T(8,128)(2,1)} %param.6), channel_id=1, source_target_pairs={{0,16},{1,17},{2,18},{3,19},{4,20},{5,21},{6,22},{7,23},{8,24},{9,... | collective-permute-start | bytes 393224 | tf_op jit(solution)/shard_map/ppermute | solution.py:12
  53.9 9.6 %copy-start = (pred[64]{0:T(512)(128)(4,1)S(1)}, pred[64]{0:T(512)(128)(4,1)}, u32[]{:S(2)}) copy-start(pred[64]{0:T(512)(128)(4,1)} %get-tuple-element.10) | copy-start | bytes 196
  58.2 4.6 %collective-permute-start.1 = (bf16[64,1024]{1,0:T(8,128)(2,1)S(1)}, bf16[64,1024]{1,0:T(8,128)(2,1)S(1)}, u32[]{:S(2)}, u32[]{:S(2)}) collective-permute-start(bf16[64,1024]{1,0:T(8,128)(2,1)S(1)} %copy.56), channel_id=1, source_target_pairs={{0,1},{1,0},{2,3},{3,2},{4,5},{5,4},{6,7},{7,6},{8,9},{9,8},{10,11... | collective-permute-start | bytes 393224 | tf_op jit(solution)/shard_map/ppermute | solution.py:12
  67.5 12.5 %collective-permute-start.2 = (bf16[64,1024]{1,0:T(8,128)(2,1)S(1)}, bf16[64,1024]{1,0:T(8,128)(2,1)S(1)}, u32[]{:S(2)}, u32[]{:S(2)}) collective-permute-start(bf16[64,1024]{1,0:T(8,128)(2,1)S(1)} %copy.64), channel_id=1, source_target_pairs={{0,256},{32,288},{64,320},{96,352},{128,384},{160,416},{192,448},{... | collective-permute-start | bytes 393224 | tf_op jit(solution)/shard_map/ppermute | solution.py:12
  80.8 9.2 %copy-start.1 = (pred[64]{0:T(512)(128)(4,1)S(1)}, pred[64]{0:T(512)(128)(4,1)}, u32[]{:S(2)}) copy-start(pred[64]{0:T(512)(128)(4,1)} %get-tuple-element.6) | copy-start | bytes 196
  82.9 6.4 %collective-permute-start.3 = (bf16[64,1024]{1,0:T(8,128)(2,1)S(1)}, bf16[64,1024]{1,0:T(8,128)(2,1)S(1)}, u32[]{:S(2)}, u32[]{:S(2)}) collective-permute-start(bf16[64,1024]{1,0:T(8,128)(2,1)S(1)} %copy.72), channel_id=1, source_target_pairs={{0,32},{32,0},{64,96},{96,64},{128,160},{160,128},{192,224},{224,1... | collective-permute-start | bytes 393224 | tf_op jit(solution)/shard_map/ppermute | solution.py:12
where the time goes:
time: 93.4 us; the launch traced here: 92.8 us
  local copies, waits for them, and re-layouts  52.1 us (56%)
  starting transfers between devices  20.2 us (22%)
  matrix products  8.62 us (9%)
  waiting for transfers between devices  7.02 us (8%)
  other arithmetic  4.39 us (5%)
    slice x2, local copies, waits for them, and re-layouts, device_rows(): return lax.dynamic_slice_in_dim(blocks[level], device * boxes, boxes, 0)  21.1 us
    ppermute x4, starting transfers between devices, from_partner(): return lax.ppermute(value, axis, pairs)  20.2 us
    ppermute x4, waiting for transfers between devices, from_partner(): return lax.ppermute(value, axis, pairs)  7.02 us
    reshape x4, local copies, waits for them, and re-layouts, combine(): self_m = self_w.reshape(boxes, R, R)  5.37 us
    dot_general x4, matrix products, combine(): jnp.einsum('bkr,bsr->bks', own_x, self_m, preferred_element_type=jnp.floa...  4.82 us
    reshape x4, local copies, waits for them, and re-layouts, combine(): other_x = picked.reshape(boxes, -1, R)  4.65 us
    convert_element_type x8, local copies, waits for them, and re-layouts, combine(): return total.reshape(boxes, -1).astype(jnp.bfloat16)  4.48 us
    reshape x4, local copies, waits for them, and re-layouts, combine(): cross_m = cross_w.reshape(boxes, R, R)  3.88 us
  transfers between devices with their start and end apart: 4, of which 2 were waited for; matrix products, arithmetic and copies ran while one was open for 49% of the time, Pallas kernels for 0%

commit v1 on v0

v1 whole, which is shorter than its diff:
```python
import functools

import jax
import jax.numpy as jnp
from jax import lax
from jax.experimental import pallas as pl
from jax.experimental.pallas import tpu as pltpu
from jax.sharding import PartitionSpec as P

R = 32
LEVELS = 4
CHUNKS = 4
ROWS = 128
MESH = pl.DeviceIdType.MESH


def iota(shape, dim):
    return lax.broadcasted_iota(jnp.int32, shape, dim)


def order_of_stages():
    offset = (0.0, 1.25, 3.85, 5.95)
    stages = [(offset[l] + 0.75 * c, l, c) for l in range(LEVELS) for c in range(CHUNKS)]
    return [(l, c) for _, l, c in sorted(stages)]


def kernel(
    n_grp, n_dev, x_hbm, self_hbm, cross_hbm, pat_hbm, o_ref,
    pat_ref, xn, wn, w, q, xs, xp, part, send, near, got, send_sem, recv_sem, load_sem,
):
    grp = lax.axis_index("grp")
    dev = lax.axis_index("dev")
    boxes = xn.shape[0]
    partner = (
        (grp, dev ^ (n_dev // 2)),
        (grp, dev ^ 1),
        (grp ^ (n_grp // 2), dev),
        (grp ^ 1, dev),
    )
    barrier = pltpu.get_barrier_semaphore()
    for level in range(LEVELS):
        pl.semaphore_signal(barrier, inc=1, device_id=partner[level], device_id_type=MESH)

    row0 = pl.multiple_of(dev * boxes, boxes)
    load_x = pltpu.make_async_copy(x_hbm, xn, load_sem.at[2 * LEVELS])
    load_x.start()
    load_pat = pltpu.make_async_copy(pat_hbm, pat_ref, load_sem.at[2 * LEVELS + 1])
    load_pat.start()
    loads = []
    for level in range(LEVELS):
        pair = []
        for kind, src in enumerate((self_hbm, cross_hbm)):
            copy = pltpu.make_async_copy(
                src.at[level, pl.ds(row0, boxes)], wn.at[level, kind], load_sem.at[2 * level + kind]
            )
            copy.start()
            pair.append(copy)
        loads.append(pair)

    load_pat.wait()
    for level in range(LEVELS):
        row = pat_ref[level, pl.ds(dev, 1), :]
        row = jnp.concatenate([row, row + boxes], axis=1)
        q[level] = (iota((ROWS, ROWS), 0) == row).astype(jnp.float32).astype(jnp.bfloat16)

    turned = iota((256, 256), 0)
    pick = ((turned % 8) * R + turned // 8 == iota((256, 256), 1)).astype(jnp.float32).astype(jnp.bfloat16)

    def prepare(level):
        for copy in loads[level]:
            copy.wait()
        for t in range(4):
            own = wn[level, 0, :, t * 256:(t + 1) * 256]
            other = wn[level, 1, :, t * 256:(t + 1) * 256]
            stack = jnp.concatenate([own, own, other, other], axis=0)
            out = lax.dot_general(
                pick, stack, (((1,), (1,)), ((), ())), preferred_element_type=jnp.float32
            )
            w[level, 0, t] = out[:, :ROWS]
            w[level, 1, t] = out[:, ROWS:]

    def stacked(ref, c):
        return jnp.concatenate(
            [ref[:, c * 256:c * 256 + 128], ref[:, c * 256 + 128:c * 256 + 256]], axis=0
        )

    def apply(level, kind, ref, accs):
        def step(r, accs):
            ws = [w[level, kind, t, pl.ds(pl.multiple_of(r * 8, 8), 8), :] for t in range(4)]
            out = []
            for k in range(4):
                x = ref[pl.ds(k * R + r, 1), :]
                out += [accs[4 * k + t] + ws[t] * x for t in range(4)]
            return tuple(out)

        return lax.fori_loop(0, R, step, tuple(accs), unroll=8)

    def self_stage(level, c):
        zero = jnp.zeros((8, ROWS), jnp.float32)
        accs = apply(level, 0, xs.at[level, c], [zero] * 16)
        for i in range(16):
            part[level, c, i * 8:(i + 1) * 8, :] = accs[i]

    def exchange(level, c):
        if level == 0:
            src = xn.at[:, pl.ds(c * 256, 256)]
            dst = near.at[:, pl.ds(c * 256, 256)]
        else:
            src = send.at[level - 1, c]
            dst = got.at[level - 1, c]
        return pltpu.make_async_remote_copy(
            src_ref=src, dst_ref=dst,
            send_sem=send_sem.at[level, c], recv_sem=recv_sem.at[level, c],
            device_id=partner[level], device_id_type=MESH,
        )

    def cross_stage(level, c):
        exchange(level, c).wait_recv()
        if level == 0:
            xp[...] = lax.dot_general(
                stacked(near, c), q[0], (((0,), (0,)), ((), ())), preferred_element_type=jnp.float32
            )
        else:
            xp[...] = jnp.dot(got[level - 1, c], q[level], preferred_element_type=jnp.float32)
        accs = apply(level, 1, xp, [part[level, c, i * 8:(i + 1) * 8, :] for i in range(16)])
        total = jnp.concatenate(accs, axis=0)
        if level < LEVELS - 1:
            total = total.astype(jnp.bfloat16)
            send[level, c] = total
            exchange(level + 1, c).start()
            xs[level + 1, c] = total.astype(jnp.float32)
            self_stage(level + 1, c)
        else:
            total = total.T.astype(jnp.bfloat16)
            o_ref[:, c * 256:c * 256 + 128] = total[:boxes]
            o_ref[:, c * 256 + 128:c * 256 + 256] = total[boxes:]

    load_x.wait()
    prepare(0)
    for c in range(CHUNKS):
        xs[0, c] = stacked(xn, c).astype(jnp.float32).T
    pl.semaphore_wait(barrier, LEVELS)
    for c in range(CHUNKS):
        exchange(0, c).start()
    for c in range(CHUNKS):
        self_stage(0, c)
    for level in range(1, LEVELS):
        prepare(level)
    for level, c in order_of_stages():
        cross_stage(level, c)
    for level in range(LEVELS):
        for c in range(CHUNKS):
            exchange(level, c).wait_send()


def shards(n_grp, n_dev, coeffs, self_blocks, cross_blocks, pattern):
    boxes, width = coeffs.shape
    bf16, f32 = jnp.bfloat16, jnp.float32
    hbm = pl.BlockSpec(memory_space=pltpu.HBM)
    vmem = pl.BlockSpec(memory_space=pltpu.VMEM)
    return pl.pallas_call(
        functools.partial(kernel, n_grp, n_dev),
        out_shape=jax.ShapeDtypeStruct((boxes, width), bf16),
        in_specs=[hbm, hbm, hbm, hbm],
        out_specs=vmem,
        scratch_shapes=[
            pltpu.VMEM(pattern.shape, jnp.int32),
            pltpu.VMEM((boxes, width), bf16),
            pltpu.VMEM((LEVELS, 2, boxes, width), bf16),
            pltpu.VMEM((LEVELS, 2, 4, 256, ROWS), f32),
            pltpu.VMEM((LEVELS, ROWS, ROWS), bf16),
            pltpu.VMEM((LEVELS, CHUNKS, ROWS, ROWS), f32),
            pltpu.VMEM((ROWS, ROWS), f32),
            pltpu.VMEM((LEVELS, CHUNKS, ROWS, ROWS), f32),
            pltpu.VMEM((LEVELS - 1, CHUNKS, ROWS, ROWS), bf16),
            pltpu.VMEM((boxes, width), bf16),
            pltpu.VMEM((LEVELS - 1, CHUNKS, ROWS, ROWS), bf16),
            pltpu.SemaphoreType.DMA((LEVELS, CHUNKS)),
            pltpu.SemaphoreType.DMA((LEVELS, CHUNKS)),
            pltpu.SemaphoreType.DMA((2 * LEVELS + 2,)),
        ],
        compiler_params=pltpu.CompilerParams(
            collective_id=0, has_side_effects=True, vmem_limit_bytes=60 * 2**20
        ),
        name="butterfly",
    )(coeffs, self_blocks, cross_blocks, pattern)


def solution(mesh):
    return jax.shard_map(
        functools.partial(shards, mesh.shape["grp"], mesh.shape["dev"]),
        mesh=mesh,
        in_specs=(
            P(("grp", "dev"), None),
            P(None, "grp", None),
            P(None, "grp", None),
            P(None, "grp", None),
        ),
        out_specs=P(("grp", "dev"), None),
        check_vma=False,
    )
```

time: 93.4 us -> 31.9 us (0.34)
  the two profiles are of different devices: /device:TPU:1 before, /device:TPU:8 now
where the time goes in v1:
time: 31.9 us; the launch traced here: 31.8 us
  Pallas kernels  30.2 us (95%)
  local copies, waits for them, and re-layouts  1.57 us (5%)
    pallas_call x1, Pallas kernels, shards(): pl.pallas_call(functools.partial(kernel, n_grp, n_dev), out_shape=jax.Sha...  30.2 us
    unnamed x1, local copies, waits for them, and re-layouts  1.57 us

profile of v1, /device:TPU:8, one launch (start us, length us, event | category | flops | bytes accessed | tf_op | source)
XLA Modules:
  0.0 31.8 jit_solution(630179090750132657)
XLA Ops:
  0.0 30.2 %butterfly.1 = bf16[64,1024]{1,0:T(8,128)(2,1)} custom-call(bf16[64,1024]{1,0:T(8,128)(2,1)} %x_hbm.1, bf16[4,2048,1024]{2,1,0:T(8,128)(2,1)} %self_hbm.1, bf16[4,2048,1024]{2,1,0:T(8,128)(2,1)} %cross_hbm.1, s32[4,32,64]{2,1,0:T(8,128)} %pat_hbm.1), custom_call_target="tpu_custom_call" | custom-call | tf_op jit(solution)/shard_map/butterfly/pallas_call | solution.py:161
  30.2 1.6 %copy.6 = bf16[64,1024]{1,0:T(8,128)(2,1)} copy(bf16[64,1024]{1,0:T(8,128)(2,1)} %butterfly.1) | data formatting | bytes 262144

commit v2 on v1

--- a/solution.py
+++ b/solution.py
@@ -19,9 +19,8 @@
 
 
 def order_of_stages():
-    offset = (0.0, 1.25, 3.85, 5.95)
-    stages = [(offset[l] + 0.75 * c, l, c) for l in range(LEVELS) for c in range(CHUNKS)]
-    return [(l, c) for _, l, c in sorted(stages)]
+    first = [(0, 0)] + [p for c in range(1, CHUNKS) for p in ((0, c), (1, c - 1))] + [(1, CHUNKS - 1)]
+    return first + [(l, c) for l in (2, 3) for c in range(CHUNKS)]
 
 
 def kernel(
@@ -57,6 +56,24 @@
             pair.append(copy)
         loads.append(pair)
 
+    def exchange(level, c):
+        if level == 0:
+            src = xn.at[:, pl.ds(c * 256, 256)]
+            dst = near.at[:, pl.ds(c * 256, 256)]
+        else:
+            src = send.at[level - 1, c]
+            dst = got.at[level - 1, c]
+        return pltpu.make_async_remote_copy(
+            src_ref=src, dst_ref=dst,
+            send_sem=send_sem.at[level, c], recv_sem=recv_sem.at[level, c],
+            device_id=partner[level], device_id_type=MESH,
+        )
+
+    load_x.wait()
+    pl.semaphore_wait(barrier, LEVELS)
+    for c in range(CHUNKS):
+        exchange(0, c).start()
+
     load_pat.wait()
     for level in range(LEVELS):
         row = pat_ref[level, pl.ds(dev, 1), :]
@@ -93,7 +110,7 @@
                 out += [accs[4 * k + t] + ws[t] * x for t in range(4)]
             return tuple(out)
 
-        return lax.fori_loop(0, R, step, tuple(accs), unroll=8)
+        return lax.fori_loop(0, R, step, tuple(accs), unroll=32)
 
     def self_stage(level, c):
         zero = jnp.zeros((8, ROWS), jnp.float32)
@@ -101,20 +118,9 @@
         for i in range(16):
             part[level, c, i * 8:(i + 1) * 8, :] = accs[i]
 
-    def exchange(level, c):
-        if level == 0:
-            src = xn.at[:, pl.ds(c * 256, 256)]
-            dst = near.at[:, pl.ds(c * 256, 256)]
-        else:
-            src = send.at[level - 1, c]
-            dst = got.at[level - 1, c]
-        return pltpu.make_async_remote_copy(
-            src_ref=src, dst_ref=dst,
-            send_sem=send_sem.at[level, c], recv_sem=recv_sem.at[level, c],
-            device_id=partner[level], device_id_type=MESH,
-        )
-
     def cross_stage(level, c):
+        if level == 2:
+            self_stage(2, c)
         exchange(level, c).wait_recv()
         if level == 0:
             xp[...] = lax.dot_general(
@@ -129,19 +135,16 @@
             send[level, c] = total
             exchange(level + 1, c).start()
             xs[level + 1, c] = total.astype(jnp.float32)
-            self_stage(level + 1, c)
+            if level != 1:
+                self_stage(level + 1, c)
         else:
             total = total.T.astype(jnp.bfloat16)
             o_ref[:, c * 256:c * 256 + 128] = total[:boxes]
             o_ref[:, c * 256 + 128:c * 256 + 256] = total[boxes:]
 
-    load_x.wait()
     prepare(0)
     for c in range(CHUNKS):
         xs[0, c] = stacked(xn, c).astype(jnp.float32).T
-    pl.semaphore_wait(barrier, LEVELS)
-    for c in range(CHUNKS):
-        exchange(0, c).start()
     for c in range(CHUNKS):
         self_stage(0, c)
     for level in range(1, LEVELS):
@@ -160,7 +163,7 @@
     vmem = pl.BlockSpec(memory_space=pltpu.VMEM)
     return pl.pallas_call(
         functools.partial(kernel, n_grp, n_dev),
-        out_shape=jax.ShapeDtypeStruct((boxes, width), bf16),
+        out_shape=pltpu.VMEM((boxes, width), bf16),
         in_specs=[hbm, hbm, hbm, hbm],
         out_specs=vmem,
         scratch_shapes=[

time: 31.9 us -> 29.5 us (0.925)
  the two profiles are of different devices: /device:TPU:8 before, /device:TPU:16 now
where the time goes in v2:
time: 29.5 us; the launch traced here: 29.4 us
  Pallas kernels  28.7 us (97%)
  local copies, waits for them, and re-layouts  0.66 us (2%)
    pallas_call x1, Pallas kernels, shards(): pl.pallas_call(functools.partial(kernel, n_grp, n_dev), out_shape=pltpu.V...  28.7 us
    unnamed x1, local copies, waits for them, and re-layouts  0.66 us

profile of v2, /device:TPU:16, one launch (start us, length us, event | category | flops | bytes accessed | tf_op | source)
XLA Modules:
  0.0 29.4 jit_solution(13330247621227578584)
XLA Ops:
  0.0 28.7 %butterfly.1 = bf16[64,1024]{1,0:T(8,128)(2,1)S(1)} custom-call(bf16[64,1024]{1,0:T(8,128)(2,1)} %x_hbm.1, bf16[4,2048,1024]{2,1,0:T(8,128)(2,1)} %self_hbm.1, bf16[4,2048,1024]{2,1,0:T(8,128)(2,1)} %cross_hbm.1, s32[4,32,64]{2,1,0:T(8,128)} %pat_hbm.1), custom_call_target="tpu_custom_call" | custom-call | tf_op jit(solution)/shard_map/butterfly/pallas_call | solution.py:164
  28.7 0.7 %copy.6 = bf16[64,1024]{1,0:T(8,128)(2,1)} copy(bf16[64,1024]{1,0:T(8,128)(2,1)S(1)} %butterfly.1) | data formatting | bytes 262144

commit v3 on v2

--- a/solution.py
+++ b/solution.py
@@ -11,6 +11,7 @@
 LEVELS = 4
 CHUNKS = 4
 ROWS = 128
+PIECES = ((0, 128), (128, 128), (256, 128), (384, 64), (448, 64))
 MESH = pl.DeviceIdType.MESH
 
 
@@ -19,8 +20,11 @@
 
 
 def order_of_stages():
-    first = [(0, 0)] + [p for c in range(1, CHUNKS) for p in ((0, c), (1, c - 1))] + [(1, CHUNKS - 1)]
-    return first + [(l, c) for l in (2, 3) for c in range(CHUNKS)]
+    first = [(0, 0)]
+    for c in range(1, CHUNKS + 1):
+        first += [(0, c)] if c < CHUNKS else []
+        first += [(1, i) for i, (at, _) in enumerate(PIECES) if at // ROWS == c - 1]
+    return first + [(l, i) for l in (2, 3) for i in range(len(PIECES))]
 
 
 def kernel(
@@ -61,8 +65,8 @@
             src = xn.at[:, pl.ds(c * 256, 256)]
             dst = near.at[:, pl.ds(c * 256, 256)]
         else:
-            src = send.at[level - 1, c]
-            dst = got.at[level - 1, c]
+            src = send.at[level - 1, pl.ds(*PIECES[c])]
+            dst = got.at[level - 1, pl.ds(*PIECES[c])]
         return pltpu.make_async_remote_copy(
             src_ref=src, dst_ref=dst,
             send_sem=send_sem.at[level, c], recv_sem=recv_sem.at[level, c],
@@ -105,54 +109,67 @@
         def step(r, accs):
             ws = [w[level, kind, t, pl.ds(pl.multiple_of(r * 8, 8), 8), :] for t in range(4)]
             out = []
-            for k in range(4):
+            for k in range(len(accs) // 4):
                 x = ref[pl.ds(k * R + r, 1), :]
                 out += [accs[4 * k + t] + ws[t] * x for t in range(4)]
             return tuple(out)
 
         return lax.fori_loop(0, R, step, tuple(accs), unroll=32)
 
-    def self_stage(level, c):
+    def self_stage(level, at, rows):
         zero = jnp.zeros((8, ROWS), jnp.float32)
-        accs = apply(level, 0, xs.at[level, c], [zero] * 16)
-        for i in range(16):
-            part[level, c, i * 8:(i + 1) * 8, :] = accs[i]
-
-    def cross_stage(level, c):
-        if level == 2:
-            self_stage(2, c)
-        exchange(level, c).wait_recv()
-        if level == 0:
-            xp[...] = lax.dot_general(
-                stacked(near, c), q[0], (((0,), (0,)), ((), ())), preferred_element_type=jnp.float32
-            )
-        else:
-            xp[...] = jnp.dot(got[level - 1, c], q[level], preferred_element_type=jnp.float32)
-        accs = apply(level, 1, xp, [part[level, c, i * 8:(i + 1) * 8, :] for i in range(16)])
+        accs = apply(level, 0, xs.at[level, pl.ds(at, rows)], [zero] * (rows // 8))
+        for i in range(rows // 8):
+            part[level, at + i * 8:at + i * 8 + 8, :] = accs[i]
+
+    def cross_piece(level, piece):
+        at, rows = PIECES[piece]
+        old = [part[level, at + i * 8:at + i * 8 + 8, :] for i in range(rows // 8)]
+        accs = apply(level, 1, xp.at[pl.ds(at % ROWS, rows)], old)
         total = jnp.concatenate(accs, axis=0)
         if level < LEVELS - 1:
             total = total.astype(jnp.bfloat16)
-            send[level, c] = total
-            exchange(level + 1, c).start()
-            xs[level + 1, c] = total.astype(jnp.float32)
+            send[level, at:at + rows, :] = total
+            exchange(level + 1, piece).start()
+            xs[level + 1, at:at + rows, :] = total.astype(jnp.float32)
             if level != 1:
-                self_stage(level + 1, c)
+                self_stage(level + 1, at, rows)
         else:
             total = total.T.astype(jnp.bfloat16)
-            o_ref[:, c * 256:c * 256 + 128] = total[:boxes]
-            o_ref[:, c * 256 + 128:c * 256 + 256] = total[boxes:]
+            for kh in range(2):
+                lane = at // ROWS * 256 + kh * ROWS + at % ROWS
+                o_ref[:, lane:lane + rows] = total[kh * boxes:(kh + 1) * boxes]
+
+    def cross_stage(level, c):
+        if level == 0:
+            exchange(0, c).wait_recv()
+            xp[...] = lax.dot_general(
+                stacked(near, c), q[0], (((0,), (0,)), ((), ())), preferred_element_type=jnp.float32
+            )
+            for piece, (at, _) in enumerate(PIECES):
+                if at // ROWS == c:
+                    cross_piece(0, piece)
+        else:
+            at, rows = PIECES[c]
+            if level == 2:
+                self_stage(2, at, rows)
+            exchange(level, c).wait_recv()
+            xp[at % ROWS:at % ROWS + rows, :] = jnp.dot(
+                got[level - 1, at:at + rows, :], q[level], preferred_element_type=jnp.float32
+            )
+            cross_piece(level, c)
 
     prepare(0)
     for c in range(CHUNKS):
-        xs[0, c] = stacked(xn, c).astype(jnp.float32).T
+        xs[0, c * ROWS:(c + 1) * ROWS, :] = stacked(xn, c).astype(jnp.float32).T
     for c in range(CHUNKS):
-        self_stage(0, c)
+        self_stage(0, c * ROWS, ROWS)
     for level in range(1, LEVELS):
         prepare(level)
     for level, c in order_of_stages():
         cross_stage(level, c)
     for level in range(LEVELS):
-        for c in range(CHUNKS):
+        for c in range(CHUNKS if level == 0 else len(PIECES)):
             exchange(level, c).wait_send()
 
 
@@ -172,14 +189,14 @@
             pltpu.VMEM((LEVELS, 2, boxes, width), bf16),
             pltpu.VMEM((LEVELS, 2, 4, 256, ROWS), f32),
             pltpu.VMEM((LEVELS, ROWS, ROWS), bf16),
-            pltpu.VMEM((LEVELS, CHUNKS, ROWS, ROWS), f32),
+            pltpu.VMEM((LEVELS, CHUNKS * ROWS, ROWS), f32),
             pltpu.VMEM((ROWS, ROWS), f32),
-            pltpu.VMEM((LEVELS, CHUNKS, ROWS, ROWS), f32),
-            pltpu.VMEM((LEVELS - 1, CHUNKS, ROWS, ROWS), bf16),
+            pltpu.VMEM((LEVELS, CHUNKS * ROWS, ROWS), f32),
+            pltpu.VMEM((LEVELS - 1, CHUNKS * ROWS, ROWS), bf16),
             pltpu.VMEM((boxes, width), bf16),
-            pltpu.VMEM((LEVELS - 1, CHUNKS, ROWS, ROWS), bf16),
-            pltpu.SemaphoreType.DMA((LEVELS, CHUNKS)),
-            pltpu.SemaphoreType.DMA((LEVELS, CHUNKS)),
+            pltpu.VMEM((LEVELS - 1, CHUNKS * ROWS, ROWS), bf16),
+            pltpu.SemaphoreType.DMA((LEVELS, len(PIECES))),
+            pltpu.SemaphoreType.DMA((LEVELS, len(PIECES))),
             pltpu.SemaphoreType.DMA((2 * LEVELS + 2,)),
         ],
         compiler_params=pltpu.CompilerParams(

time: 29.5 us -> 29.7 us (level)
  no operation moved by 1% of the time
where the time goes in v3:
time: 29.7 us; the launch traced here: 29.6 us
  Pallas kernels  28.9 us (97%)
  local copies, waits for them, and re-layouts  0.66 us (2%)
    pallas_call x1, Pallas kernels, shards(): pl.pallas_call(functools.partial(kernel, n_grp, n_dev), out_shape=pltpu.V...  28.9 us
    unnamed x1, local copies, waits for them, and re-layouts  0.66 us

profile of v3, /device:TPU:16, one launch (start us, length us, event | category | flops | bytes accessed | tf_op | source)
XLA Modules:
  0.0 29.6 jit_solution(1309573248623745356)
XLA Ops:
  0.0 28.9 %butterfly.1 = bf16[64,1024]{1,0:T(8,128)(2,1)S(1)} custom-call(bf16[64,1024]{1,0:T(8,128)(2,1)} %x_hbm.1, bf16[4,2048,1024]{2,1,0:T(8,128)(2,1)} %self_hbm.1, bf16[4,2048,1024]{2,1,0:T(8,128)(2,1)} %cross_hbm.1, s32[4,32,64]{2,1,0:T(8,128)} %pat_hbm.1), custom_call_target="tpu_custom_call" | custom-call | tf_op jit(solution)/shard_map/butterfly/pallas_call | solution.py:181
  28.9 0.7 %copy.6 = bf16[64,1024]{1,0:T(8,128)(2,1)} copy(bf16[64,1024]{1,0:T(8,128)(2,1)S(1)} %butterfly.1) | data formatting | bytes 262144

commit v4 on v2

--- a/solution.py
+++ b/solution.py
@@ -58,7 +58,7 @@
 
     def exchange(level, c):
         if level == 0:
-            src = xn.at[:, pl.ds(c * 256, 256)]
+            src = x_hbm.at[:, pl.ds(c * 256, 256)]
             dst = near.at[:, pl.ds(c * 256, 256)]
         else:
             src = send.at[level - 1, c]
@@ -69,10 +69,10 @@
             device_id=partner[level], device_id_type=MESH,
         )
 
-    load_x.wait()
     pl.semaphore_wait(barrier, LEVELS)
     for c in range(CHUNKS):
         exchange(0, c).start()
+    load_x.wait()
 
     load_pat.wait()
     for level in range(LEVELS):

time: 29.5 us -> 29.5 us (level)
  no operation moved by 1% of the time
where the time goes in v4:
time: 29.5 us; the launch traced here: 29.4 us
  Pallas kernels  28.7 us (97%)
  local copies, waits for them, and re-layouts  0.66 us (2%)
    pallas_call x1, Pallas kernels, shards(): pl.pallas_call(functools.partial(kernel, n_grp, n_dev), out_shape=pltpu.V...  28.7 us
    unnamed x1, local copies, waits for them, and re-layouts  0.66 us

profile of v4, /device:TPU:16, one launch (start us, length us, event | category | flops | bytes accessed | tf_op | source)
XLA Modules:
  0.0 29.4 jit_solution(1481982956888209397)
XLA Ops:
  0.0 28.7 %butterfly.1 = bf16[64,1024]{1,0:T(8,128)(2,1)S(1)} custom-call(bf16[64,1024]{1,0:T(8,128)(2,1)} %x_hbm.1, bf16[4,2048,1024]{2,1,0:T(8,128)(2,1)} %self_hbm.1, bf16[4,2048,1024]{2,1,0:T(8,128)(2,1)} %cross_hbm.1, s32[4,32,64]{2,1,0:T(8,128)} %pat_hbm.1), custom_call_target="tpu_custom_call" | custom-call | tf_op jit(solution)/shard_map/butterfly/pallas_call | solution.py:164
  28.7 0.7 %copy.6 = bf16[64,1024]{1,0:T(8,128)(2,1)} copy(bf16[64,1024]{1,0:T(8,128)(2,1)S(1)} %butterfly.1) | data formatting | bytes 262144
